TPU v7x, 256 devices: a whole 4x4x8 slice. The times are simulated.
256 devices in a mesh: occ: 32 (over z, y), vir: 8 (over x, core).
Axes of the slice: x: 4, y: 4, z: 8, core: 2. Of those that a mesh axis runs over, the one named last changes fastest.
Arguments:
- amplitudes: bfloat16 [256, 32, 128, 128], P('occ', None, 'vir'), may hold values from -6 to 6
- integrals: bfloat16 [64, 32, 128, 128], P('occ', 'vir'), may hold values from -0.09375 to 0.09375
- tile_list: int32 [256, 32], P('occ'), may hold values from 0 to 63, as said below
- counts: int32 [256], P('occ'), may hold values from 1 to 32, 5120 in all
Outputs:
- ladder: bfloat16 [256, 32, 128, 128], P('occ', 'vir')
Inputs may be any that keep to these rules, and one draw needn't show every extreme that they name: `tile_list`: within one pair block the 32 entries are distinct. Slots 0 to counts[b] - 1 of block b are live; some block has all 32 live.
All inputs are finite; a program needn't handle non-finite values.
Results may differ from a plain program's by a relative error of at most 0.001.
Values may be sent and summed in bfloat16 or wider, within the bound.
A program may use at most 128 MiB of HBM per device.

v0:
```python
import jax
import jax.numpy as jnp
from jax import lax
from jax.sharding import PartitionSpec as P


def on_device(amplitudes, integrals, tile_list, counts):
    gathered = lax.all_gather(amplitudes, "vir", axis=2, tiled=True)
    slots = tile_list.shape[1]
    live = jnp.arange(slots, dtype=jnp.int32)[None, :] < counts[:, None]
    piece = lax.all_gather(integrals, "occ", axis=0, tiled=True)
    columns = jnp.arange(piece.shape[0], dtype=jnp.int32)
    selector = ((tile_list[:, :, None] == columns[None, None, :]) & live[:, :, None]).astype(
        jnp.bfloat16
    )
    expanded = jnp.einsum(
        "bsc,bspt->bcpt", selector, gathered, preferred_element_type=jnp.float32
    ).astype(jnp.bfloat16)
    ladder = jnp.einsum("bcpt,catu->bapu", expanded, piece, preferred_element_type=jnp.float32)
    return ladder.astype(jnp.bfloat16)


def solution(mesh):
    placed = (P("occ", None, "vir", None), P("occ", "vir", None, None), P("occ", None), P("occ"))
    return jax.shard_map(
        on_device,
        mesh=mesh,
        in_specs=placed,
        out_specs=P("occ", "vir", None, None),
        check_vma=False,
    )
```

profile of v0, /device:TPU:1, one launch (start us, length us, event | category | flops | bytes accessed | tf_op | source)
XLA Modules:
  0.0 192.3 jit_solution(6793013997033518295)
XLA Ops:
  6.5 0.0 all-gather.3.cloned.1.call-start
  6.5 0.7 all-gather.3.cloned.1.call-update
  7.3 0.0 all-gather.5.cloned.1.call-start
  7.3 1.7 copy.5
  9.0 0.0 all-gather.5.cloned.1.call-update
  9.0 0.7 iota_compare_fusion.1
  9.7 60.2 %all-gather.3.cloned.1.call-done = bf16[8,32,128,128]{3,2,1,0:T(8,128)(2,1)} async-done(((bf16[8,32,16,128]{3,2,1,0:T(8,128)(2,1)}), bf16[8,32,128,128]{3,2,1,0:T(8,128)(2,1)}) %all-gather.3.cloned.1.call-update) | async-done | bytes 8388624 | tf_op jit(solution)/shard_map/all_gather | solution.py:8
  69.9 14.8 %fusion.4 = bf16[8,64,128,128]{3,1,2,0:T(8,128)(2,1)} fusion(bf16[8,32,128,128]{3,2,1,0:T(8,128)(2,1)} %all-gather.3.cloned.1.call-done, s32[8,32]{1,0:T(8,128)} %param.6, pred[8,32]{1,0:T(8,128)(4,1)S(1)} %iota_compare_fusion.1), kind=kOutput, calls=%fused_computation.4 | convolution fusion | flops 536903680 | bytes 25167104 | tf_op jit(solution)/shard_map/bsc,bspt->bcpt/dot_general | solution.py:16
  84.7 86.5 %all-gather.5.cloned.1.call-done = bf16[64,4,128,128]{3,2,0,1:T(8,128)(2,1)} async-done(((bf16[2,4,128,128]{3,2,0,1:T(8,128)(2,1)}), bf16[64,4,128,128]{3,2,0,1:T(8,128)(2,1)}) %all-gather.5.cloned.1.call-update) | async-done | bytes 8388624 | tf_op jit(solution)/shard_map/all_gather | solution.py:11
  171.2 14.3 %fusion.10 = bf16[8,4,128,128]{3,2,1,0:T(8,128)(2,1)} fusion(bf16[64,4,128,128]{3,2,0,1:T(8,128)(2,1)} %all-gather.5.cloned.1.call-done, bf16[8,64,128,128]{3,1,2,0:T(8,128)(2,1)} %fusion.4), kind=kOutput, calls=%fused_computation.7 | convolution fusion | flops 8590458880 | bytes 26214400 | tf_op jit(solution)/shard_map/bcpt,catu->bapu/dot_general | solution.py:19
Async XLA Ops:
  6.5 63.4 %all-gather.3.cloned.1.call-start = ((), (), s32[]{:S(2)}) async-start(), calls=%async_computation | async-start | bytes 9437184 | tf_op jit(solution)/shard_map/all_gather | solution.py:8
  7.3 163.9 %all-gather.5.cloned.1.call-start = ((), (), s32[]{:S(2)}) async-start(), calls=%async_computation.1 | async-start | bytes 8650752 | tf_op jit(solution)/shard_map/all_gather | solution.py:11
Sparse Core Ops, SparseCore 0:
  9.2 60.6 all-gather.2
  72.5 98.6 all-gather.4
where the time goes:
time: 192 us
  waiting for transfers between devices  147 us (77%)
  matrix products  29.1 us (15%)
  between operations  13.4 us (7%)
    all_gather x1, waiting for transfers between devices, on_device(): piece = lax.all_gather(integrals, 'occ', axis=0, tiled=True)  86.5 us
    all_gather x1, waiting for transfers between devices, on_device(): gathered = lax.all_gather(amplitudes, 'vir', axis=2, tiled=True)  60.2 us
    dot_general x1, matrix products, on_device(): jnp.einsum('bsc,bspt->bcpt', selector, gathered, preferred_element_type=j...  14.8 us
    dot_general x1, matrix products, on_device(): jnp.einsum('bcpt,catu->bapu', expanded, piece, preferred_element_type=jnp...  14.3 us
  transfers between devices with their start and end apart: 2, of which 2 were waited for; matrix products, arithmetic and copies ran while one was open for 9% of the time, Pallas kernels for 0%

commit v1 on v0

v1 whole, which is shorter than its diff:
```python
import collections
import functools
import heapq
import itertools

import jax
import jax.numpy as jnp
from jax import lax
from jax.experimental import pallas as pl
from jax.experimental.pallas import tpu as pltpu
from jax.sharding import PartitionSpec as P

MESH = pl.DeviceIdType.MESH
NX, NY, NZ = 4, 4, 8
TILE, SLOTS, NB, NA = 128, 32, 8, 4
ROWS = 2 * NA * TILE
SPLIT = 416
ROW_NS, HOP_NS, HANDLER_NS, RELAY_NS = 5.6, 2400.0, 80.0, 2500.0
QUEUE_NS = {"x": 9000.0, "y": 3500.0, "z": 3500.0}
LARGE_NS, BLOCK_NS, SMALL_NS = 170.0, 145.0, 460.0
Z_RANK, Y_RANK = (2, 0.5, -2, -2), (3, -0.5, 1, 2)
HALVES = {1: (None,), 2: (None,)}
GROUPS = (4, 2, 2)
LAST_DY = (0, 1, 3, 2)
LATE = 24
VMEM_KIB = 48 * 2**10


def part_rows(part, half):
    start, rows = (0, SPLIT) if part == 1 else (SPLIT, ROWS - SPLIT)
    if half is None:
        return start, rows
    cut = rows // 2 // 16 * 16
    return (start, cut) if half == 0 else (start + cut, rows - cut)


def group_of(block):
    first = 0
    for g, size in enumerate(GROUPS):
        if block < first + size:
            return g, block - first
        first += size


def plan():
    free, ready, heap, count = collections.defaultdict(float), collections.defaultdict(list), [], itertools.count()
    steps, now = [], 0.0
    large = [(g, dz % NZ) for dz in (0, 1, -1, 2, -2, 3, -3) for g in range(len(GROUPS))]
    small = list(LAST_DY)
    rows_left = {(dz, dy): ROWS for dz in range(NZ) for dy in range(NY)}
    rows_left[0, 0] = 0
    blocks_left, blocks_at = [4 * size for size in GROUPS], [0.0] * len(GROUPS)

    def side(direction):
        return 0 if direction > 0 else 1

    def add(part, dz, dy, half, axis, direction):
        dz, dy = (dz - direction, dy) if axis == "z" else (dz, dy - direction)
        weights = Z_RANK if axis == "z" else Y_RANK
        rank = sum(w * v for w, v in zip(weights, (abs(dz), abs(dy), part == 2, half is not None)))
        piece = ("i", part, dz, dy, half, axis, direction)
        ready[axis, direction].append((rank, next(count), part_rows(part, half)[1], piece))

    def add_block(block, stage, direction):
        rank = block if stage == 2 else NB + block
        rows = SLOTS * 16 // stage
        ready["x", direction].append((rank, next(count), rows, ("a", block, stage, direction)))

    def sends():
        out, more = [], True
        while more:
            more = False
            for link in [(axis, direction) for axis in "yzx" for direction in (1, -1)]:
                if ready[link] and free[link] - now < QUEUE_NS[link[0]]:
                    item = min(ready[link])
                    ready[link].remove(item)
                    free[link] = max(now, free[link]) + item[2] * ROW_NS
                    heapq.heappush(heap, (free[link] + HOP_NS, next(count), item[3]))
                    out.append(item[3])
                    more = True
        return out

    for direction in (1, -1):
        for part in (1, 2):
            for half in HALVES[part]:
                add(part, 0, 0, half, "y", direction)
                add(part, 0, 0, half, "z", direction)
        for block in range(NB):
            add_block(block, 1, direction)
    steps.append((None, sends()))
    while heap or small:
        while small and (not heap or heap[0][0] > now):
            able = [g for g in range(len(GROUPS)) if not blocks_left[g] and (blocks_at[g] <= now or not heap)]
            fit = [u for u in large if u[0] in able and not any(rows_left[u[1], dy] for dy in range(NY))]
            if fit:
                large.remove(fit[0])
                now = max(now, blocks_at[fit[0][0]]) + LARGE_NS + BLOCK_NS * GROUPS[fit[0][0]]
                steps.append((("large", *fit[0]), sends()))
            elif not large and not rows_left[NZ // 2, small[0]]:
                now += SMALL_NS
                steps.append((("small", small.pop(0)), sends()))
            else:
                break
        if not heap:
            continue
        at, _, piece = heapq.heappop(heap)
        now = max(now, at) + HANDLER_NS
        if piece[0] == "a":
            _, block, stage, direction = piece
            if stage == 1:
                add_block(block, 2, direction)
            g = group_of(block)[0]
            blocks_left[g] -= 1
            blocks_at[g] = now + RELAY_NS
        else:
            _, part, dz, dy, half, axis, direction = piece
            rows_left[dz % NZ, dy % NY] -= part_rows(part, half)[1]
            hops, last = (abs(dz), NZ // 2) if axis == "z" else (abs(dy), NY // 2)
            if hops < last - 1:
                add(part, dz, dy, half, axis, direction)
            elif hops == last - 1 and half in (None, side(direction)):
                add(part, dz, dy, side(direction), axis, direction)
            if (part, axis) in ((1, "y"), (2, "z")):
                for turn in (1, -1):
                    add(part, dz, dy, half, "z" if axis == "y" else "y", turn)
        steps.append((piece, sends()))
    return steps


def kernel(steps, amp, ints, tiles_hbm, counts_hbm, result, blocks0, blocks1, blocks2, pieces, lhs, total, tiles, counts, slot_v,
           slot_s, send_sem, recv_sem, relay_send, relay_recv, local_sem):
    occ, vir = lax.axis_index("occ"), lax.axis_index("vir")
    x, core, z, y = vir // 2, vir % 2, occ // NY, occ % NY
    blocks = (blocks0, blocks1, blocks2)

    def near(axis, d):
        if axis == "x":
            return {"vir": (x + d + NX) % NX * 2 + core}
        if axis == "y":
            return {"occ": z * NY + (y + d + NY) % NY}
        return {"occ": (z + d + NZ) % NZ * NY + y}

    partner = {"vir": x * 2 + 1 - core}
    barrier = pltpu.get_barrier_semaphore()
    for device in [partner] + [near(axis, d) for axis in "xyz" for d in (1, -1)]:
        pl.semaphore_signal(barrier, inc=1, device_id=device, device_id_type=MESH)
    pl.semaphore_wait(barrier, 7)

    def vir_at(d, c):
        return (x + d + NX) % NX * 2 + c

    def block_at(owner, b, half=None):
        slots = pl.ds(0, SLOTS) if half is None else pl.ds(half * (SLOTS // 2), SLOTS // 2)
        g, place = group_of(b)
        return blocks[g].at[owner, place, slots]

    def side(d):
        return 0 if d > 0 else 1

    order = [piece for _, sent in steps for piece in sent]
    number = {piece: i for i, piece in enumerate(order)}

    def copy(piece, arriving=False):
        i = number[piece]
        if piece[0] == "a":
            _, b, stage, d = piece
            axis = "x"
            if stage == 1:
                src, dst = amp.at[b], block_at(vir_at(-d, core) if arriving else vir, b)
            else:
                src = block_at(vir_at(-d, core), b, side(d))
                dst = block_at(vir_at(2, core), b, side(d)) if arriving else src
        else:
            _, part, dz, dy, half, axis, d = piece
            rows = pl.ds(*part_rows(part, half))
            oz, oy = (dz + d, dy) if axis == "z" else (dz, dy + d)
            src = ints.at[rows] if (oz, oy) == (0, 0) else pieces.at[oz % NZ, oy % NY, rows]
            dst = pieces.at[dz % NZ, dy % NY, rows]
        return pltpu.make_async_remote_copy(
            src, dst, send_sem.at[i], recv_sem.at[i], device_id=near(axis, d), device_id_type=MESH
        )

    relays = [("own", b) for b in range(NB)] + [piece for piece in order if piece[0] == "a"]
    relay_number = {piece: i for i, piece in enumerate(relays)}

    def relay(piece, arriving=False):
        i = relay_number[piece]
        c = 1 - core if arriving else core
        if piece[0] == "own":
            dst = block_at(vir_at(0, c), piece[1])
            src = amp.at[piece[1]]
        else:
            _, b, stage, d = piece
            dst = block_at(vir_at(-d, c), b) if stage == 1 else block_at(vir_at(2, c), b, side(d))
            src = dst
        return pltpu.make_async_remote_copy(
            src, dst, relay_send.at[i], relay_recv.at[i], device_id=partner, device_id_type=MESH
        )

    own_blocks = [pltpu.make_async_copy(amp.at[b], block_at(vir, b), local_sem.at[b]) for b in range(NB)]
    own_piece = pltpu.make_async_copy(ints, pieces.at[0, 0], local_sem.at[NB])

    def prepare():
        lists = [
            pltpu.make_async_copy(tiles_hbm, tiles, local_sem.at[NB + 4]),
            pltpu.make_async_copy(counts_hbm, counts, local_sem.at[NB + 5]),
        ]
        for read in lists:
            read.start()
        own_piece.start()
        for b in range(NB):
            own_blocks[b].start()
            relay(("own", b)).start()
        for read in lists:
            read.wait()
        lane = lax.broadcasted_iota(jnp.int32, (NB, 128), 1)
        row = lax.broadcasted_iota(jnp.int32, (NB, 128), 0)
        tile = 2 * ((z + lane // 8) % NZ * NY + (y + lane // 2 % 4) % NY) + lane % 2
        live = jnp.zeros((NB, 128), jnp.int32)
        for b in range(NB):
            live = jnp.where(row == b, counts[b], live)
        slot = jnp.full((NB, 128), SLOTS, jnp.int32)
        listed = tiles[...]
        for s in range(SLOTS):
            slot = jnp.where((listed[:, s : s + 1] == tile) & (live > s), s, slot)
        slot_v[...] = slot
        to_scalars = pltpu.make_async_copy(slot_v, slot_s, local_sem.at[NB + 1])
        to_scalars.start()
        for group, size in zip(blocks, GROUPS):
            group[:, :, SLOTS] = jnp.zeros((2 * NX, size, 16, TILE), jnp.bfloat16)
        total[...] = jnp.zeros_like(total)
        to_scalars.wait()

    def group_ready(g):
        for b in range(NB):
            if group_of(b)[0] == g:
                own_blocks[b].wait()
        for piece in relays:
            if group_of(piece[1])[0] == g:
                relay(piece, True).wait_recv()

    rounds, units = [[]], []
    for event, sent in steps:
        if event is not None and event[0] in ("large", "small"):
            units.append(event)
            rounds.append([])
            event = None
        rounds[-1].append((event, sent))
    large = [u[1:] for u in units if u[0] == "large"]

    def run_round(r):
        for i, (event, sent) in enumerate(rounds[r]):
            if event is not None:
                copy(event, True).wait_recv()
            for piece in sent:
                copy(piece).start()
            if event is not None and event[0] == "a":
                relay(event).start()
            if r == 0 and i == 0:
                prepare()
        if r == 0:
            own_piece.wait()
        for g in range(len(GROUPS)):
            if r == [u[0] for u in large].index(g):
                group_ready(g)

    def gather(b, dz):
        g, place = group_of(b)
        found = [slot_s[b, dz * 8 + q] for q in range(8)]
        return jnp.concatenate([blocks[g][:, place, s].reshape(TILE, TILE) for s in found], axis=1)

    def origin(dz, dy):
        return jnp.concatenate(
            [
                jnp.concatenate([pieces[dz, dy, pl.ds((j * NA + a) * TILE, TILE)] for a in range(NA)], axis=1)
                for j in range(2)
            ],
            axis=0,
        )

    def run_large(g, dz):
        mine = [b for b in range(NB) if group_of(b)[0] == g]
        left = jnp.concatenate([gather(b, dz) for b in mine], axis=0)
        right = jnp.concatenate([origin(dz, dy) for dy in range(NY)], axis=0)
        here = pl.ds(mine[0] * TILE, len(mine) * TILE)
        total[here] += jnp.dot(left, right, preferred_element_type=jnp.float32)

    @pl.loop(0, len(large))
    def _(u):
        for r in range(len(large)):
            pl.when(u == r)(functools.partial(run_round, r))
        group, dz = jnp.int32(0), jnp.int32(0)
        for r, (g, d) in enumerate(large):
            group, dz = jnp.where(u == r, g, group), jnp.where(u == r, d, dz)
        for g in range(len(GROUPS)):
            pl.when(group == g)(functools.partial(run_large, g, dz))

    for b in range(NB):
        lhs[pl.ds(b * TILE, TILE)] = gather(b, NZ // 2)
    for u in range(len(large), len(units)):
        last = u == len(units) - 1
        if last:
            for piece in order[:-LATE]:
                copy(piece).wait_send()
            for piece in relays:
                relay(piece).wait_send()
        run_round(u)
        dy = units[u][1]
        sums = total[...] + jnp.dot(
            lhs[:, 2 * dy * TILE : 2 * (dy + 1) * TILE], origin(NZ // 2, dy), preferred_element_type=jnp.float32
        )
        if not last:
            total[...] = sums
            continue
        for b in range(NB):
            for a in range(NA):
                tile = sums[b * TILE : (b + 1) * TILE, a * TILE : (a + 1) * TILE]
                result[b, a] = tile.astype(jnp.bfloat16)
    for piece in order[-LATE:]:
        copy(piece).wait_send()


def on_device(amplitudes, integrals, tile_list, counts):
    steps = plan()
    operands = (amplitudes, integrals.reshape(ROWS, TILE), tile_list, counts)
    copies = sum(len(sent) for _, sent in steps)
    return pl.pallas_call(
        functools.partial(kernel, steps),
        out_shape=pltpu.VMEM((NB, NA, TILE, TILE), jnp.bfloat16),
        in_specs=[pl.BlockSpec(memory_space=pltpu.HBM)] * 4,
        out_specs=pl.BlockSpec(memory_space=pltpu.VMEM),
        scratch_shapes=[
            *[pltpu.VMEM((2 * NX, size, SLOTS + 1, 16, TILE), jnp.bfloat16) for size in GROUPS],
            pltpu.VMEM((NZ, NY, ROWS, TILE), jnp.bfloat16),
            pltpu.VMEM((NB * TILE, 8 * TILE), jnp.bfloat16),
            pltpu.VMEM((NB * TILE, NA * TILE), jnp.float32),
            pltpu.VMEM((NB, SLOTS), jnp.int32),
            pltpu.SMEM((NB,), jnp.int32),
            pltpu.VMEM((NB, 128), jnp.int32),
            pltpu.SMEM((NB, 128), jnp.int32),
            pltpu.SemaphoreType.DMA((copies,)),
            pltpu.SemaphoreType.DMA((copies,)),
            pltpu.SemaphoreType.DMA((5 * NB,)),
            pltpu.SemaphoreType.DMA((5 * NB,)),
            pltpu.SemaphoreType.DMA((NB + 6,)),
        ],
        compiler_params=pltpu.CompilerParams(
            collective_id=0, has_side_effects=True, vmem_limit_bytes=VMEM_KIB * 2**10
        ),
    )(*[pltpu.with_memory_space_constraint(x, pltpu.HBM) for x in operands])


def solution(mesh):
    placed = (P("occ", None, "vir", None), P("occ", "vir", None, None), P("occ", None), P("occ"))
    return jax.shard_map(
        on_device,
        mesh=mesh,
        in_specs=placed,
        out_specs=P("occ", "vir", None, None),
        check_vma=False,
    )
```

time: 192 us -> 60.9 us (0.32)
  waiting for transfers between devices: 147 us -> 0 us
  Pallas kernels: 0 us -> 59.7 us
  matrix products: 29.1 us -> 0 us
  between operations: 13.4 us -> 0.01 us
    all_gather x2 -> x0, waiting for transfers between devices: 147 us -> none  [the longest x1 86.5 us: on_device(): piece = lax.all_gather(integrals, 'occ', axis=0, tiled=True)]
    pallas_call x0 -> x1, Pallas kernels: none -> 59.7 us  [on_device(): pl.pallas_call(functools.partial(kernel, steps), out_shape=pltpu.VMEM((NB...]
    dot_general x2 -> x0, matrix products: 29.1 us -> none  [the longest x1 14.8 us: on_device(): jnp.einsum('bsc,bspt->bcpt', selector, gathered, preferred_element_type=j...]
  transfers between devices with their start and end apart: 2 -> 0, of which waited for: 2 -> 0; matrix products, arithmetic and copies ran while one was open for 9% -> 0% of each run, Pallas kernels for 0% -> 0%
where the time goes in v1:
time: 60.9 us; the launch traced here: 60.7 us
  Pallas kernels  59.7 us (98%)
  local copies, waits for them, and re-layouts  0.97 us (2%)
    pallas_call x1, Pallas kernels, on_device(): pl.pallas_call(functools.partial(kernel, steps), out_shape=pltpu.VMEM((NB...  59.7 us

profile of v1, /device:TPU:1, one launch (start us, length us, event | category | flops | bytes accessed | tf_op | source)
XLA Modules:
  0.0 60.7 jit_solution(1122352341716093571)
XLA Ops:
  0.0 59.7 %shard_map.46 = bf16[8,4,128,128]{3,2,1,0:T(8,128)(2,1)S(1)} custom-call(bf16[8,32,16,128]{3,2,1,0:T(8,128)(2,1)} %amp.1, bf16[1024,128]{1,0:T(8,128)(2,1)} %bitcast.1, s32[8,32]{1,0:T(8,128)} %tiles_hbm.1, s32[8]{0:T(128)} %counts_hbm.1), custom_call_target="tpu_custom_call" | custom-call | tf_op jit(solution)/shard_map/pallas_call | solution.py:327
  59.7 1.0 %copy.6 = bf16[8,4,128,128]{3,2,1,0:T(8,128)(2,1)} copy(bf16[8,4,128,128]{3,2,1,0:T(8,128)(2,1)S(1)} %shard_map.46) | data formatting | bytes 2097152

commit v2 on v1

--- a/solution.py
+++ b/solution.py
@@ -15,13 +15,13 @@
 TILE, SLOTS, NB, NA = 128, 32, 8, 4
 ROWS = 2 * NA * TILE
 SPLIT = 416
-ROW_NS, HOP_NS, HANDLER_NS, RELAY_NS = 5.6, 2400.0, 80.0, 2500.0
+ROW_NS, HOP_NS, HANDLER_NS, RELAY_NS = 5.6, 2400.0, 80.0, 1500.0
 QUEUE_NS = {"x": 9000.0, "y": 3500.0, "z": 3500.0}
 LARGE_NS, BLOCK_NS, SMALL_NS = 170.0, 145.0, 460.0
 Z_RANK, Y_RANK = (2, 0.5, -2, -2), (3, -0.5, 1, 2)
 HALVES = {1: (None,), 2: (None,)}
 GROUPS = (4, 2, 2)
-LAST_DY = (0, 1, 3, 2)
+EARLY, LATER = (0, 1, -1, 2, -2), (3, -3, 4)
 LATE = 24
 VMEM_KIB = 48 * 2**10
 
@@ -45,8 +45,8 @@
 def plan():
     free, ready, heap, count = collections.defaultdict(float), collections.defaultdict(list), [], itertools.count()
     steps, now = [], 0.0
-    large = [(g, dz % NZ) for dz in (0, 1, -1, 2, -2, 3, -3) for g in range(len(GROUPS))]
-    small = list(LAST_DY)
+    large = [(g, dz % NZ) for dz in EARLY for g in range(len(GROUPS))]
+    small = [(dz % NZ, dy) for dz in LATER for dy in (0, 1, 3, 2)]
     rows_left = {(dz, dy): ROWS for dz in range(NZ) for dy in range(NY)}
     rows_left[0, 0] = 0
     blocks_left, blocks_at = [4 * size for size in GROUPS], [0.0] * len(GROUPS)
@@ -96,11 +96,13 @@
                 large.remove(fit[0])
                 now = max(now, blocks_at[fit[0][0]]) + LARGE_NS + BLOCK_NS * GROUPS[fit[0][0]]
                 steps.append((("large", *fit[0]), sends()))
-            elif not large and not rows_left[NZ // 2, small[0]]:
-                now += SMALL_NS
-                steps.append((("small", small.pop(0)), sends()))
-            else:
+                continue
+            fit = [u for u in small if len(able) == len(GROUPS) and not rows_left[u]]
+            if not fit:
                 break
+            small.remove(fit[0])
+            now += SMALL_NS
+            steps.append((("small", *fit[0]), sends()))
         if not heap:
             continue
         at, _, piece = heapq.heappop(heap)
@@ -127,7 +129,7 @@
     return steps
 
 
-def kernel(steps, amp, ints, tiles_hbm, counts_hbm, result, blocks0, blocks1, blocks2, pieces, lhs, total, tiles, counts, slot_v,
+def kernel(steps, amp, ints, tiles_hbm, counts_hbm, result, blocks0, blocks1, blocks2, pieces, total, tiles, counts, slot_v,
            slot_s, send_sem, recv_sem, relay_send, relay_recv, local_sem):
     occ, vir = lax.axis_index("occ"), lax.axis_index("vir")
     x, core, z, y = vir // 2, vir % 2, occ // NY, occ % NY
@@ -246,7 +248,7 @@
             rounds.append([])
             event = None
         rounds[-1].append((event, sent))
-    large = [u[1:] for u in units if u[0] == "large"]
+    first_use = [[u[:2] for u in units].index(("large", g)) for g in range(len(GROUPS))]
 
     def run_round(r):
         for i, (event, sent) in enumerate(rounds[r]):
@@ -261,12 +263,12 @@
         if r == 0:
             own_piece.wait()
         for g in range(len(GROUPS)):
-            if r == [u[0] for u in large].index(g):
+            if r == first_use[g]:
                 group_ready(g)
 
-    def gather(b, dz):
+    def gather(b, dz, tiles):
         g, place = group_of(b)
-        found = [slot_s[b, dz * 8 + q] for q in range(8)]
+        found = [slot_s[b, dz * 8 + q] for q in tiles]
         return jnp.concatenate([blocks[g][:, place, s].reshape(TILE, TILE) for s in found], axis=1)
 
     def origin(dz, dy):
@@ -280,42 +282,46 @@
 
     def run_large(g, dz):
         mine = [b for b in range(NB) if group_of(b)[0] == g]
-        left = jnp.concatenate([gather(b, dz) for b in mine], axis=0)
+        left = jnp.concatenate([gather(b, dz, range(8)) for b in mine], axis=0)
         right = jnp.concatenate([origin(dz, dy) for dy in range(NY)], axis=0)
         here = pl.ds(mine[0] * TILE, len(mine) * TILE)
         total[here] += jnp.dot(left, right, preferred_element_type=jnp.float32)
 
-    @pl.loop(0, len(large))
-    def _(u):
-        for r in range(len(large)):
-            pl.when(u == r)(functools.partial(run_round, r))
-        group, dz = jnp.int32(0), jnp.int32(0)
-        for r, (g, d) in enumerate(large):
-            group, dz = jnp.where(u == r, g, group), jnp.where(u == r, d, dz)
-        for g in range(len(GROUPS)):
-            pl.when(group == g)(functools.partial(run_large, g, dz))
-
+    def run_small(dz, dy):
+        left = jnp.concatenate([gather(b, dz, (2 * dy, 2 * dy + 1)) for b in range(NB)], axis=0)
+        return total[...] + jnp.dot(left, origin(dz, dy), preferred_element_type=jnp.float32)
+
+    def run_units(first, stop):
+        @pl.loop(first, stop)
+        def _(u):
+            dz = jnp.int32(0)
+            for r in range(first, stop):
+                pl.when(u == r)(functools.partial(run_round, r))
+                dz = jnp.where(u == r, units[r][2], dz)
+            run_large(units[first][1], dz)
+
+    u = 0
+    while u < len(units) - 1:
+        if units[u][0] == "small":
+            run_round(u)
+            total[...] = run_small(*units[u][1:])
+            u += 1
+            continue
+        stop = u + 1
+        while units[stop][:2] == units[u][:2]:
+            stop += 1
+        run_units(u, stop)
+        u = stop
+
+    for piece in order[:-LATE]:
+        copy(piece).wait_send()
+    for piece in relays:
+        relay(piece).wait_send()
+    run_round(len(units) - 1)
+    sums = run_small(*units[-1][1:])
     for b in range(NB):
-        lhs[pl.ds(b * TILE, TILE)] = gather(b, NZ // 2)
-    for u in range(len(large), len(units)):
-        last = u == len(units) - 1
-        if last:
-            for piece in order[:-LATE]:
-                copy(piece).wait_send()
-            for piece in relays:
-                relay(piece).wait_send()
-        run_round(u)
-        dy = units[u][1]
-        sums = total[...] + jnp.dot(
-            lhs[:, 2 * dy * TILE : 2 * (dy + 1) * TILE], origin(NZ // 2, dy), preferred_element_type=jnp.float32
-        )
-        if not last:
-            total[...] = sums
-            continue
-        for b in range(NB):
-            for a in range(NA):
-                tile = sums[b * TILE : (b + 1) * TILE, a * TILE : (a + 1) * TILE]
-                result[b, a] = tile.astype(jnp.bfloat16)
+        for a in range(NA):
+            result[b, a] = sums[b * TILE : (b + 1) * TILE, a * TILE : (a + 1) * TILE].astype(jnp.bfloat16)
     for piece in order[-LATE:]:
         copy(piece).wait_send()
 
@@ -332,7 +338,6 @@
         scratch_shapes=[
             *[pltpu.VMEM((2 * NX, size, SLOTS + 1, 16, TILE), jnp.bfloat16) for size in GROUPS],
             pltpu.VMEM((NZ, NY, ROWS, TILE), jnp.bfloat16),
-            pltpu.VMEM((NB * TILE, 8 * TILE), jnp.bfloat16),
             pltpu.VMEM((NB * TILE, NA * TILE), jnp.float32),
             pltpu.VMEM((NB, SLOTS), jnp.int32),
             pltpu.SMEM((NB,), jnp.int32),

time: 60.9 us -> 59.3 us (0.974)
  Pallas kernels: 59.7 us -> 58.3 us
    pallas_call x1, Pallas kernels: 59.7 us -> 58.3 us  [on_device(): pl.pallas_call(functools.partial(kernel, steps), out_shape=pltpu.VMEM((NB...]
where the time goes in v2:
time: 59.3 us; the launch traced here: 59.2 us
  Pallas kernels  58.3 us (98%)
  local copies, waits for them, and re-layouts  0.97 us (2%)
    pallas_call x1, Pallas kernels, on_device(): pl.pallas_call(functools.partial(kernel, steps), out_shape=pltpu.VMEM((NB...  58.3 us

profile of v2, /device:TPU:1, one launch (start us, length us, event | category | flops | bytes accessed | tf_op | source)
XLA Modules:
  0.0 59.2 jit_solution(328701948453813452)
XLA Ops:
  0.0 58.3 %shard_map.46 = bf16[8,4,128,128]{3,2,1,0:T(8,128)(2,1)S(1)} custom-call(bf16[8,32,16,128]{3,2,1,0:T(8,128)(2,1)} %amp.1, bf16[1024,128]{1,0:T(8,128)(2,1)} %bitcast.1, s32[8,32]{1,0:T(8,128)} %tiles_hbm.1, s32[8]{0:T(128)} %counts_hbm.1), custom_call_target="tpu_custom_call" | custom-call | tf_op jit(solution)/shard_map/pallas_call | solution.py:333
  58.3 1.0 %copy.6 = bf16[8,4,128,128]{3,2,1,0:T(8,128)(2,1)} copy(bf16[8,4,128,128]{3,2,1,0:T(8,128)(2,1)S(1)} %shard_map.46) | data formatting | bytes 2097152

commit v3 on v2

--- a/solution.py
+++ b/solution.py
@@ -15,13 +15,14 @@
 TILE, SLOTS, NB, NA = 128, 32, 8, 4
 ROWS = 2 * NA * TILE
 SPLIT = 416
-ROW_NS, HOP_NS, HANDLER_NS, RELAY_NS = 5.6, 2400.0, 80.0, 1500.0
-QUEUE_NS = {"x": 9000.0, "y": 3500.0, "z": 3500.0}
-LARGE_NS, BLOCK_NS, SMALL_NS = 170.0, 145.0, 460.0
-Z_RANK, Y_RANK = (2, 0.5, -2, -2), (3, -0.5, 1, 2)
+ROW_NS, HOP_NS, HANDLER_NS, RELAY_NS = 5.6, 1900.0, 80.0, 1500.0
+QUEUE_NS = {"x": 5500.0, "y": 3500.0, "z": 4500.0}
+LARGE_NS, BLOCK_NS, SMALL_NS, PAIR_NS, SINGLE_NS = 170.0, 145.0, 460.0, 740.0, 0.0
+Z_RANK, Y_RANK = (2, 0.5, -2, 0), (0.5, -0.5, 1, -1)
 HALVES = {1: (None,), 2: (None,)}
 GROUPS = (4, 2, 2)
 EARLY, LATER = (0, 1, -1, 2, -2), (3, -3, 4)
+TOGETHER = 2
 LATE = 24
 VMEM_KIB = 48 * 2**10
 
@@ -100,9 +101,12 @@
             fit = [u for u in small if len(able) == len(GROUPS) and not rows_left[u]]
             if not fit:
                 break
-            small.remove(fit[0])
-            now += SMALL_NS
-            steps.append((("small", *fit[0]), sends()))
+            if len(fit) == 1 and len(small) > 1 and heap and heap[0][0] < now + SINGLE_NS:
+                break
+            fit = fit[:TOGETHER]
+            small = [u for u in small if u not in fit]
+            now += SMALL_NS if len(fit) == 1 else PAIR_NS
+            steps.append((("small", *fit), sends()))
         if not heap:
             continue
         at, _, piece = heapq.heappop(heap)
@@ -144,7 +148,7 @@
 
     partner = {"vir": x * 2 + 1 - core}
     barrier = pltpu.get_barrier_semaphore()
-    for device in [partner] + [near(axis, d) for axis in "xyz" for d in (1, -1)]:
+    for device in [near(axis, d) for axis in "zyx" for d in (1, -1)] + [partner]:
         pl.semaphore_signal(barrier, inc=1, device_id=device, device_id_type=MESH)
     pl.semaphore_wait(barrier, 7)
 
@@ -287,9 +291,16 @@
         here = pl.ds(mine[0] * TILE, len(mine) * TILE)
         total[here] += jnp.dot(left, right, preferred_element_type=jnp.float32)
 
-    def run_small(dz, dy):
-        left = jnp.concatenate([gather(b, dz, (2 * dy, 2 * dy + 1)) for b in range(NB)], axis=0)
-        return total[...] + jnp.dot(left, origin(dz, dy), preferred_element_type=jnp.float32)
+    def run_small(*origins):
+        left = jnp.concatenate(
+            [
+                jnp.concatenate([gather(b, dz, (2 * dy, 2 * dy + 1)) for b in range(NB)], axis=0)
+                for dz, dy in origins
+            ],
+            axis=1,
+        )
+        right = jnp.concatenate([origin(dz, dy) for dz, dy in origins], axis=0)
+        return total[...] + jnp.dot(left, right, preferred_element_type=jnp.float32)
 
     def run_units(first, stop):
         @pl.loop(first, stop)

time: 59.3 us -> 58.5 us (0.987)
  Pallas kernels: 58.3 us -> 57.2 us
    pallas_call x1, Pallas kernels: 58.3 us -> 57.2 us  [on_device(): pl.pallas_call(functools.partial(kernel, steps), out_shape=pltpu.VMEM((NB...]
where the time goes in v3:
time: 58.5 us; the launch traced here: 58.2 us
  Pallas kernels  57.2 us (98%)
  local copies, waits for them, and re-layouts  0.97 us (2%)
    pallas_call x1, Pallas kernels, on_device(): pl.pallas_call(functools.partial(kernel, steps), out_shape=pltpu.VMEM((NB...  57.2 us

profile of v3, /device:TPU:1, one launch (start us, length us, event | category | flops | bytes accessed | tf_op | source)
XLA Modules:
  0.0 58.2 jit_solution(11377919894436651161)
XLA Ops:
  0.0 57.2 %shard_map.46 = bf16[8,4,128,128]{3,2,1,0:T(8,128)(2,1)S(1)} custom-call(bf16[8,32,16,128]{3,2,1,0:T(8,128)(2,1)} %amp.1, bf16[1024,128]{1,0:T(8,128)(2,1)} %bitcast.1, s32[8,32]{1,0:T(8,128)} %tiles_hbm.1, s32[8]{0:T(128)} %counts_hbm.1), custom_call_target="tpu_custom_call" | custom-call | tf_op jit(solution)/shard_map/pallas_call | solution.py:344
  57.2 1.0 %copy.6 = bf16[8,4,128,128]{3,2,1,0:T(8,128)(2,1)} copy(bf16[8,4,128,128]{3,2,1,0:T(8,128)(2,1)S(1)} %shard_map.46) | data formatting | bytes 2097152

commit v4 on v3

--- a/solution.py
+++ b/solution.py
@@ -133,7 +133,7 @@
     return steps
 
 
-def kernel(steps, amp, ints, tiles_hbm, counts_hbm, result, blocks0, blocks1, blocks2, pieces, total, tiles, counts, slot_v,
+def kernel(steps, amp, ints, tiles_hbm, counts_hbm, total, last_left, last_right, blocks0, blocks1, blocks2, pieces, tiles, counts, slot_v,
            slot_s, send_sem, recv_sem, relay_send, relay_recv, local_sem):
     occ, vir = lax.axis_index("occ"), lax.axis_index("vir")
     x, core, z, y = vir // 2, vir % 2, occ // NY, occ % NY
@@ -291,16 +291,20 @@
         here = pl.ds(mine[0] * TILE, len(mine) * TILE)
         total[here] += jnp.dot(left, right, preferred_element_type=jnp.float32)
 
-    def run_small(*origins):
-        left = jnp.concatenate(
+    def left_of(origins):
+        return jnp.concatenate(
             [
                 jnp.concatenate([gather(b, dz, (2 * dy, 2 * dy + 1)) for b in range(NB)], axis=0)
                 for dz, dy in origins
             ],
             axis=1,
         )
-        right = jnp.concatenate([origin(dz, dy) for dz, dy in origins], axis=0)
-        return total[...] + jnp.dot(left, right, preferred_element_type=jnp.float32)
+
+    def right_of(origins):
+        return jnp.concatenate([origin(dz, dy) for dz, dy in origins], axis=0)
+
+    def run_small(*origins):
+        return total[...] + jnp.dot(left_of(origins), right_of(origins), preferred_element_type=jnp.float32)
 
     def run_units(first, stop):
         @pl.loop(first, stop)
@@ -328,28 +332,46 @@
         copy(piece).wait_send()
     for piece in relays:
         relay(piece).wait_send()
+    last_left[...] = left_of(units[-1][1:])
     run_round(len(units) - 1)
-    sums = run_small(*units[-1][1:])
-    for b in range(NB):
-        for a in range(NA):
-            result[b, a] = sums[b * TILE : (b + 1) * TILE, a * TILE : (a + 1) * TILE].astype(jnp.bfloat16)
+    last_right[...] = right_of(units[-1][1:])
     for piece in order[-LATE:]:
         copy(piece).wait_send()
 
 
+def write_out(sums, left, right, out, rounded, sems):
+    writes = []
+    for first in range(0, NB, 2):
+        rows = pl.ds(first * TILE, 2 * TILE)
+        chunk = sums[rows] + jnp.dot(left[rows], right[...], preferred_element_type=jnp.float32)
+        for b in range(2):
+            for a in range(NA):
+                tile = chunk[b * TILE : (b + 1) * TILE, a * TILE : (a + 1) * TILE]
+                rounded[first + b, a] = tile.astype(jnp.bfloat16)
+        here = pl.ds(first, 2)
+        writes.append(pltpu.make_async_copy(rounded.at[here], out.at[here], sems.at[first]))
+        writes[-1].start()
+    for write in writes:
+        write.wait()
+
+
 def on_device(amplitudes, integrals, tile_list, counts):
     steps = plan()
+    depth = 2 * TILE * (len([e for e, _ in steps if e is not None and e[0] == "small"][-1]) - 1)
     operands = (amplitudes, integrals.reshape(ROWS, TILE), tile_list, counts)
     copies = sum(len(sent) for _, sent in steps)
-    return pl.pallas_call(
+    parts = pl.pallas_call(
         functools.partial(kernel, steps),
-        out_shape=pltpu.VMEM((NB, NA, TILE, TILE), jnp.bfloat16),
+        out_shape=[
+            pltpu.VMEM((NB * TILE, NA * TILE), jnp.float32),
+            pltpu.VMEM((NB * TILE, depth), jnp.bfloat16),
+            pltpu.VMEM((depth, NA * TILE), jnp.bfloat16),
+        ],
         in_specs=[pl.BlockSpec(memory_space=pltpu.HBM)] * 4,
-        out_specs=pl.BlockSpec(memory_space=pltpu.VMEM),
+        out_specs=[pl.BlockSpec(memory_space=pltpu.VMEM)] * 3,
         scratch_shapes=[
             *[pltpu.VMEM((2 * NX, size, SLOTS + 1, 16, TILE), jnp.bfloat16) for size in GROUPS],
             pltpu.VMEM((NZ, NY, ROWS, TILE), jnp.bfloat16),
-            pltpu.VMEM((NB * TILE, NA * TILE), jnp.float32),
             pltpu.VMEM((NB, SLOTS), jnp.int32),
             pltpu.SMEM((NB,), jnp.int32),
             pltpu.VMEM((NB, 128), jnp.int32),
@@ -364,6 +386,13 @@
             collective_id=0, has_side_effects=True, vmem_limit_bytes=VMEM_KIB * 2**10
         ),
     )(*[pltpu.with_memory_space_constraint(x, pltpu.HBM) for x in operands])
+    return pl.pallas_call(
+        write_out,
+        out_shape=pltpu.HBM((NB, NA, TILE, TILE), jnp.bfloat16),
+        in_specs=[pl.BlockSpec(memory_space=pltpu.VMEM)] * 3,
+        out_specs=pl.BlockSpec(memory_space=pl.ANY),
+        scratch_shapes=[pltpu.VMEM((NB, NA, TILE, TILE), jnp.bfloat16), pltpu.SemaphoreType.DMA((NB,))],
+    )(*[pltpu.with_memory_space_constraint(x, pltpu.VMEM) for x in parts])
 
 
 def solution(mesh):

time: 58.5 us -> 58.3 us (level)
  local copies, waits for them, and re-layouts: 0.97 us -> 0 us
  Pallas kernels: 57.2 us -> 58 us
    unnamed x1 -> x0, local copies, waits for them, and re-layouts: 0.97 us -> none
    pallas_call x1 -> x2, Pallas kernels: 57.2 us -> 58 us  [the longest x1 56.7 us: on_device(): pl.pallas_call(functools.partial(kernel, steps), out_shape=[pltpu.VMEM((N...]
where the time goes in v4:
time: 58.3 us; the launch traced here: 58 us
  Pallas kernels  58 us (99%)
    pallas_call x1, Pallas kernels, on_device(): pl.pallas_call(functools.partial(kernel, steps), out_shape=[pltpu.VMEM((N...  56.7 us
    pallas_call x1, Pallas kernels, on_device(): pl.pallas_call(write_out, out_shape=pltpu.HBM((NB, NA, TILE, TILE), jnp.b...  1.27 us

profile of v4, /device:TPU:1, one launch (start us, length us, event | category | flops | bytes accessed | tf_op | source)
XLA Modules:
  0.0 58.0 jit_solution(15482932325870142027)
XLA Ops:
  0.0 56.7 %shard_map.46 = (f32[1024,512]{1,0:T(8,128)S(1)}, bf16[1024,256]{1,0:T(8,128)(2,1)S(1)}, bf16[256,512]{1,0:T(8,128)(2,1)S(1)}) custom-call(bf16[8,32,16,128]{3,2,1,0:T(8,128)(2,1)} %amp.1, bf16[1024,128]{1,0:T(8,128)(2,1)} %bitcast.1, s32[8,32]{1,0:T(8,128)} %tiles_hbm.1, s32[8]{0:T(128)} %counts_hbm.1), custom_call_target="tpu_custom_call" | custom-call | tf_op jit(solution)/shard_map/pallas_call | solution.py:363
  56.8 1.3 %shard_map.47 = bf16[8,4,128,128]{3,2,1,0:T(8,128)(2,1)} custom-call(f32[1024,512]{1,0:T(8,128)S(1)} %get-tuple-element.8.sums, bf16[1024,256]{1,0:T(8,128)(2,1)S(1)} %get-tuple-element.9.left, bf16[256,512]{1,0:T(8,128)(2,1)S(1)} %get-tuple-element.10.right), custom_call_target="tpu_custom_call" | custom-call | tf_op jit(solution)/shard_map/pallas_call | solution.py:389

commit v5 on v4

--- a/solution.py
+++ b/solution.py
@@ -341,14 +341,14 @@
 
 def write_out(sums, left, right, out, rounded, sems):
     writes = []
-    for first in range(0, NB, 2):
-        rows = pl.ds(first * TILE, 2 * TILE)
+    for first, size in ((0, 1), (1, 2), (3, 2), (5, 2), (7, 1)):
+        rows = pl.ds(first * TILE, size * TILE)
         chunk = sums[rows] + jnp.dot(left[rows], right[...], preferred_element_type=jnp.float32)
-        for b in range(2):
+        for b in range(size):
             for a in range(NA):
                 tile = chunk[b * TILE : (b + 1) * TILE, a * TILE : (a + 1) * TILE]
                 rounded[first + b, a] = tile.astype(jnp.bfloat16)
-        here = pl.ds(first, 2)
+        here = pl.ds(first, size)
         writes.append(pltpu.make_async_copy(rounded.at[here], out.at[here], sems.at[first]))
         writes[-1].start()
     for write in writes:

time: 58.3 us -> 58.3 us (level)
  no operation moved by 1% of the time
where the time goes in v5:
time: 58.3 us; the launch traced here: 58 us
  Pallas kernels  58 us (99%)
    pallas_call x1, Pallas kernels, on_device(): pl.pallas_call(functools.partial(kernel, steps), out_shape=[pltpu.VMEM((N...  56.7 us
    pallas_call x1, Pallas kernels, on_device(): pl.pallas_call(write_out, out_shape=pltpu.HBM((NB, NA, TILE, TILE), jnp.b...  1.26 us

profile of v5, /device:TPU:1, one launch (start us, length us, event | category | flops | bytes accessed | tf_op | source)
XLA Modules:
  0.0 58.0 jit_solution(10360082374924340717)
XLA Ops:
  0.0 56.7 %shard_map.46 = (f32[1024,512]{1,0:T(8,128)S(1)}, bf16[1024,256]{1,0:T(8,128)(2,1)S(1)}, bf16[256,512]{1,0:T(8,128)(2,1)S(1)}) custom-call(bf16[8,32,16,128]{3,2,1,0:T(8,128)(2,1)} %amp.1, bf16[1024,128]{1,0:T(8,128)(2,1)} %bitcast.1, s32[8,32]{1,0:T(8,128)} %tiles_hbm.1, s32[8]{0:T(128)} %counts_hbm.1), custom_call_target="tpu_custom_call" | custom-call | tf_op jit(solution)/shard_map/pallas_call | solution.py:363
  56.8 1.3 %shard_map.47 = bf16[8,4,128,128]{3,2,1,0:T(8,128)(2,1)} custom-call(f32[1024,512]{1,0:T(8,128)S(1)} %get-tuple-element.8.sums, bf16[1024,256]{1,0:T(8,128)(2,1)S(1)} %get-tuple-element.9.left, bf16[256,512]{1,0:T(8,128)(2,1)S(1)} %get-tuple-element.10.right), custom_call_target="tpu_custom_call" | custom-call | tf_op jit(solution)/shard_map/pallas_call | solution.py:389
